TPU v7x, 32 devices: a whole 2x2x4 slice. The times are simulated.
32 devices in a mesh: expert: 8 (over y, x, core), dp: 4 (over z).
Axes of the slice: x: 2, y: 2, z: 4, core: 2. Of those that a mesh axis runs over, the one named last changes fastest.
Arguments:
- attn_input: bfloat16 [3072, 4096], P('dp'), may hold values from -6 to 6
- query_grad: bfloat16 [3072, 8192], P('dp', 'expert'), may hold values from -6 to 6
- query_weight: float32 [8192, 4096], P(('expert', 'dp')), may hold values from -40 to 40
- moe_cotangent: bfloat16 [1024, 4096], P('expert', 'dp'), may hold values from -6 to 6
- expert_ids: int32 [1024, 8], P('expert'), may hold values from 0 to 15, all different within a row; in each aligned block of 128 rows (0 to 127, 128 to 255, ...) at most 80 rows name the same one
- route_weights: float32 [1024, 8], P('expert'), may hold values from 0.2 to 1
- gate_saved: bfloat16 [640, 16, 1536], P('dp', 'expert'), may hold values from -6 to 6
- up_saved: bfloat16 [640, 16, 1536], P('dp', 'expert'), may hold values from -6 to 6
- gate_weight: bfloat16 [16, 4096, 1536], P('expert', 'dp'), may hold values from -0.09375 to 0.09375
- up_weight: bfloat16 [16, 4096, 1536], P('expert', 'dp'), may hold values from -0.09375 to 0.09375
- down_weight: bfloat16 [16, 1536, 4096], P('expert', None, 'dp'), may hold values from -0.15625 to 0.15625
Outputs:
- query_weight_next: float32 [8192, 4096], P(('expert', 'dp'))
- moe_input_grad: float32 [1024, 4096], P('expert', 'dp')
Inputs may be any that keep to these rules, and one draw needn't show every extreme that they name: `expert_ids`: in each aligned block of 128 rows no expert is named by more than 80 rows, and one expert by exactly 80 rows in some block; each row names 8 different experts.
All inputs are finite; a program needn't handle non-finite values.
Results may differ from a plain program's by a relative error of at most 0.022.
Values may be sent and summed in bfloat16 or wider, within the bound.
No kernel may reach another device: no remote copies, remote signals or barrier semaphores. Data moves between devices by JAX's collectives and lax.ppermute only.
A program may use at most 128 MiB of HBM per device.

v0:
```python
import jax
import jax.numpy as jnp
from jax import lax
from jax.sharding import PartitionSpec as P

step_rate = 0.01
epsilon = 1e-06


def slot_tables(expert_ids, route_weights, experts, capacity):
    expert_iota = lax.broadcasted_iota(jnp.int32, (1, 1, experts), 2)
    chosen = (expert_ids[:, :, None] == expert_iota).astype(jnp.int32)
    counts = jnp.sum(chosen, axis=1, dtype=jnp.int32)
    before = jnp.cumsum(counts, axis=0, dtype=jnp.int32) - counts
    position = jnp.sum(chosen * before[:, None, :], axis=2, dtype=jnp.int32)
    slot_code = position * experts + expert_ids
    slot_iota = lax.broadcasted_iota(jnp.int32, (1, 1, capacity * experts), 2)
    matched = slot_code[:, :, None] == slot_iota
    select = jnp.sum(matched.astype(jnp.float32), axis=1)
    scaled = jnp.sum(jnp.where(matched, route_weights[:, :, None], 0.0), axis=1)
    return (select, scaled)


def activation_grads(hidden, gate_vals, up_vals):
    gate_float = gate_vals.astype(jnp.float32)
    up_float = up_vals.astype(jnp.float32)
    sigmoid_vals = jax.nn.sigmoid(gate_float)
    gate_grad = hidden * up_float * sigmoid_vals * (1.0 + gate_float * (1.0 - sigmoid_vals))
    up_grad = hidden * gate_float * sigmoid_vals
    return jnp.stack([gate_grad, up_grad], axis=2).astype(jnp.bfloat16)


def weight_update(attn_input, query_grad, query_weight):
    gradient = lax.psum_scatter(
        lax.dot_general(
            query_grad, attn_input, (((0,), (0,)), ((), ())), preferred_element_type=jnp.float32
        ).astype(jnp.bfloat16),
        "dp",
        scatter_dimension=0,
        tiled=True,
    ).astype(jnp.float32)
    radial = jnp.mean(query_weight * gradient, axis=1, keepdims=True) / (
        jnp.mean(query_weight * query_weight, axis=1, keepdims=True) + epsilon
    )
    stepped = query_weight - step_rate * (gradient - radial * query_weight)
    return stepped * lax.rsqrt(jnp.mean(stepped * stepped, axis=1, keepdims=True) + epsilon)


def expert_update(
    moe_cotangent,
    expert_ids,
    route_weights,
    gate_saved,
    up_saved,
    gate_weight,
    up_weight,
    down_weight,
):
    groups = lax.axis_size("expert")
    experts = gate_weight.shape[0] * groups
    capacity = gate_saved.shape[0] * lax.axis_size("dp") // groups
    select, scaled = slot_tables(expert_ids, route_weights, experts, capacity)
    outgoing = jnp.dot(
        scaled.T,
        moe_cotangent.astype(jnp.float32),
        precision=lax.Precision.HIGHEST,
        preferred_element_type=jnp.float32,
    )
    outgoing = outgoing.astype(jnp.bfloat16).reshape(capacity, experts, moe_cotangent.shape[1])
    arrived = lax.all_to_all(outgoing, "expert", split_axis=1, concat_axis=0, tiled=True)
    hidden = lax.psum_scatter(
        jnp.einsum("sec,ehc->seh", arrived, down_weight, preferred_element_type=jnp.float32).astype(
            jnp.bfloat16
        ),
        "dp",
        scatter_dimension=0,
        tiled=True,
    ).astype(jnp.float32)
    grads_pair = activation_grads(hidden, gate_saved, up_saved)
    part_rows = lax.all_gather(grads_pair, "dp", axis=0, tiled=True)
    total = jnp.einsum(
        "seh,ech->sec", part_rows[:, :, 0], gate_weight, preferred_element_type=jnp.float32
    )
    total = total + jnp.einsum(
        "seh,ech->sec", part_rows[:, :, 1], up_weight, preferred_element_type=jnp.float32
    )
    slot_input = total.astype(jnp.bfloat16)
    returned_rows = lax.all_to_all(slot_input, "expert", split_axis=0, concat_axis=1, tiled=True)
    flat_rows = returned_rows.reshape(capacity * experts, returned_rows.shape[2])
    return jnp.dot(select.astype(jnp.bfloat16), flat_rows, preferred_element_type=jnp.float32)


def shards(
    attn_input,
    query_grad,
    query_weight,
    moe_cotangent,
    expert_ids,
    route_weights,
    gate_saved,
    up_saved,
    gate_weight,
    up_weight,
    down_weight,
):
    moe_input_grad = expert_update(
        moe_cotangent,
        expert_ids,
        route_weights,
        gate_saved,
        up_saved,
        gate_weight,
        up_weight,
        down_weight,
    )
    query_weight_next = weight_update(attn_input, query_grad, query_weight)
    return (query_weight_next, moe_input_grad)


def solution(mesh):
    placed = (
        P("dp", None),
        P("dp", "expert"),
        P(("expert", "dp"), None),
        P("expert", "dp"),
        P("expert", None),
        P("expert", None),
        P("dp", "expert", None),
        P("dp", "expert", None),
        P("expert", "dp", None),
        P("expert", "dp", None),
        P("expert", None, "dp"),
    )
    return jax.shard_map(
        shards,
        mesh=mesh,
        in_specs=placed,
        out_specs=(P(("expert", "dp"), None), P("expert", "dp")),
        check_vma=False,
    )
```

profile of v0, /device:TPU:0, one launch (start us, length us, event | category | flops | bytes accessed | tf_op | source)
XLA Modules:
  0.0 455.0 jit_solution(4535292178305415681)
XLA Ops:
  7.2 0.8 convert_reduce_fusion.1
  8.0 0.1 copy.35
  8.1 0.2 reduce_window_sum.11
  8.4 0.7 select_reduce_fusion.1
  9.1 0.7 multiply_add_fusion
  9.8 0.1 copy.38
  9.9 0.8 copy.39
  10.7 3.4 convert_reduce_fusion
  14.1 3.2 convolution_convert_fusion.2
  17.3 1.4 copy.40
  18.8 37.3 %all_to_all.33 = bf16[80,16,1024]{2,0,1:T(8,128)(2,1)S(1)} all-to-all(bf16[80,16,1024]{2,0,1:T(8,128)(2,1)S(1)} %copy.40), channel_id=1, replica_groups=mesh['expert'=8,'dp'=4] {'expert'}, dimensions={1} | all-to-all | bytes 5242880 | tf_op jit(solution)/shard_map/all_to_all | solution.py:70
  56.1 0.3 copy.41
  56.4 5.8 %fusion.5 = bf16[640,2,1536]{2,0,1:T(8,128)(2,1)} fusion(bf16[640,2,1024]{2,0,1:T(8,128)(2,1)S(1)} %bitcast.38, bf16[2,1536,1024]{2,1,0:T(8,128)(2,1)S(1)} %bitcast.40), kind=kOutput, calls=%fused_computation.18 | convolution fusion | flops 4028497920 | bytes 12845056 | tf_op jit(solution)/shard_map/sec,ehc->seh/dot_general | solution.py:72
  62.3 72.2 %reduce-scatter.5.cloned.1.call-done = bf16[160,2,1536]{2,0,1:T(8,128)(2,1)} async-done(((bf16[640,2,1536]{2,0,1:T(8,128)(2,1)}), bf16[160,2,1536]{2,0,1:T(8,128)(2,1)}) %reduce-scatter.5.cloned.1.call-update) | async-done | bytes 983056 | tf_op jit(solution)/shard_map/reduce_scatter | solution.py:71
  134.4 2.5 fusion.18
  137.0 1.4 pad_maximum_fusion
  138.4 0.2 reduce-scatter.3.cloned.1.call-start
  138.7 11.8 %convolution_convert_fusion = bf16[1024,4096]{1,0:T(8,128)(2,1)} fusion(bf16[768,1024]{1,0:T(8,128)(2,1)S(1)} %copy-done, bf16[768,4096]{1,0:T(8,128)(2,1)} %param.11), kind=kOutput, calls=%fused_computation | convolution fusion | flops 6446645248 | bytes 16252928 | tf_op jit(solution)/shard_map/dot_general | solution.py:35
  150.4 129.5 %all-gather.2.cloned.1.call-done = bf16[640,2,2,1536]{3,0,1,2:T(8,128)(2,1)} async-done(((bf16[160,2,2,1536]{3,0,1,2:T(8,128)(2,1)}), bf16[640,2,2,1536]{3,0,1,2:T(8,128)(2,1)}) %all-gather.2.cloned.1.call-update) | async-done | bytes 7864336 | tf_op jit(solution)/shard_map/all_gather | solution.py:80
  280.0 7.6 %fusion.3 = f32[2,640,1024]{2,1,0:T(8,128)S(1)} fusion(bf16[2,1024,1536]{2,1,0:T(8,128)(2,1)} %param.20, bf16[640,2,2,1536]{3,0,1,2:T(8,128)(2,1)} %all-gather.2.cloned.1.call-done), kind=kOutput, calls=%fused_computation.14 | convolution fusion | flops 4026531840 | bytes 15466496 | tf_op jit(solution)/shard_map/seh,ech->sec/dot_general | solution.py:84
  287.6 8.2 %fusion.6 = bf16[640,2,1024]{2,0,1:T(8,128)(2,1)S(1)} fusion(f32[2,640,1024]{2,1,0:T(8,128)S(1)} %fusion.3, bf16[2,1024,1536]{2,1,0:T(8,128)(2,1)} %param.19, bf16[640,2,2,1536]{3,0,1,2:T(8,128)(2,1)} %all-gather.2.cloned.1.call-done), kind=kOutput, calls=%fused_computation.22 | convolution fusion | flops 4029153280 | bytes 18087936 | tf_op jit(solution)/shard_map/seh,ech->sec/dot_general | solution.py:81
  295.8 4.3 copy.44
  300.1 4.6 %all-to-all-start.1 = ((bf16[640,2,1024]{2,1,0:T(2,128)(2,1)}), bf16[640,2,1024]{2,1,0:T(2,128)(2,1)}, u32[]{:S(2)}, u32[]{:S(2)}) async-start(bf16[640,2,1024]{2,1,0:T(2,128)(2,1)} %copy.44), calls=%async_computation.3 | async-start | bytes 5242880 | tf_op jit(solution)/shard_map/all_to_all | solution.py:88
  304.7 120.3 %reduce-scatter.3.cloned.1.call-done = bf16[256,4096]{1,0:T(8,128)(2,1)} async-done(((bf16[1024,4096]{1,0:T(8,128)(2,1)}), bf16[256,4096]{1,0:T(8,128)(2,1)}) %reduce-scatter.3.cloned.1.call-update) | async-done | bytes 2097168 | tf_op jit(solution)/shard_map/reduce_scatter | solution.py:34
  425.0 3.9 fusion
  428.9 0.1 copy-done.2
  429.1 0.7 copy-done.3
  429.8 1.1 multiply_reduce_fusion
  430.9 3.1 fusion.7
  434.0 6.2 %copy.52 = bf16[8,80,2,1024]{3,2,0,1:T(2,128)(2,1)} copy(bf16[8,80,2,1024]{3,2,1,0:T(2,128)(2,1)} %bitcast.10) | data formatting | bytes 5242880 | tf_op jit(solution)/shard_map/all_to_all | solution.py:88
  440.1 5.3 %reshape.44 = bf16[1280,1024]{1,0:T(8,128)(2,1)} reshape(bf16[80,8,2,1024]{3,2,1,0:T(2,128)(2,1)} %bitcast.37) | data formatting | bytes 5242880 | tf_op jit(solution)/shard_map/reshape | solution.py:89
  445.4 3.0 fusion.21
  (23 shorter events, 0.2 us)
Async XLA Ops:
  7.2 131.5 %copy-start = (bf16[768,1024]{1,0:T(8,128)(2,1)S(1)}, bf16[768,1024]{1,0:T(8,128)(2,1)}, u32[]{:S(2)}) copy-start(bf16[768,1024]{1,0:T(8,128)(2,1)} %param.12) | copy-start | bytes 4718596
  7.2 127.3 %reduce-scatter.5.cloned.1.call-start = ((), (), s32[]{:S(2)}) async-start(), calls=%async_computation.5 | async-start | bytes 4915200 | tf_op jit(solution)/shard_map/reduce_scatter | solution.py:71
  17.3 39.1 %slice-start = ((s8[6291456]{0:T(1024)(128)(4,1)}), s8[4194304]{0:T(1024)(128)(4,1)S(1)}, s32[]{:S(2)}) async-start(s8[6291456]{0:T(1024)(128)(4,1)} %bitcast.39), calls=%async_computation.7 | async-start | bytes 8388608
  18.8 37.6 %slice-start.1 = ((s8[6291456]{0:T(1024)(128)(4,1)}), s8[2097152]{0:T(1024)(128)(4,1)S(1)}, s32[]{:S(2)}) async-start(s8[6291456]{0:T(1024)(128)(4,1)} %bitcast.39), calls=%async_computation.8 | async-start | bytes 4194304
  62.2 72.2 %copy-start.4 = (bf16[160,2,1536]{2,1,0:T(2,128)(2,1)S(1)}, bf16[160,2,1536]{2,1,0:T(2,128)(2,1)}, u32[]{:S(2)}) copy-start(bf16[160,2,1536]{2,1,0:T(2,128)(2,1)} %param.18) | copy-start | bytes 2949124
  62.2 217.7 %all-gather.2.cloned.1.call-start = ((), (), s32[]{:S(2)}) async-start(), calls=%async_computation.6 | async-start | bytes 9830400 | tf_op jit(solution)/shard_map/all_gather | solution.py:80
  138.4 286.6 %reduce-scatter.3.cloned.1.call-start = ((), (), s32[]{:S(2)}) async-start(), calls=%async_computation.4 | async-start | bytes 10485760 | tf_op jit(solution)/shard_map/reduce_scatter | solution.py:34
  300.1 133.9 %all-to-all-start.1 = ((bf16[640,2,1024]{2,1,0:T(2,128)(2,1)}), bf16[640,2,1024]{2,1,0:T(2,128)(2,1)}, u32[]{:S(2)}, u32[]{:S(2)}) async-start(bf16[640,2,1024]{2,1,0:T(2,128)(2,1)} %copy.44), calls=%async_computation.3 | async-start | bytes 5242880 | tf_op jit(solution)/shard_map/all_to_all | solution.py:88
  425.0 4.1 copy-start.2
  425.0 4.7 %copy-start.3 = (bf16[256,4096]{1,0:T(8,128)(2,1)S(1)}, bf16[256,4096]{1,0:T(8,128)(2,1)}, u32[]{:S(2)}) copy-start(bf16[256,4096]{1,0:T(8,128)(2,1)} %reduce-scatter.3.cloned.1.call-done) | copy-start | bytes 6291460
  440.1 8.3 %copy-start.1 = (bf16[768,1024]{1,0:T(8,128)(2,1)S(1)}, bf16[768,1024]{1,0:T(8,128)(2,1)}, u32[]{:S(2)}) copy-start(bf16[768,1024]{1,0:T(8,128)(2,1)} %param.12) | copy-start | bytes 4718596
Sparse Core Ops, SparseCore 0:
  62.3 72.0 reduce-scatter.4
  138.5 141.3 all-gather.1
  282.3 142.6 reduce-scatter.2
where the time goes:
time: 456 us; the launch traced here: 455 us
  waiting for transfers between devices  322 us (71%)
  matrix products  39.6 us (9%)
  blocking collectives  37.3 us (8%)
  local copies, waits for them, and re-layouts  19.3 us (4%)
  other arithmetic  17.9 us (4%)
  between operations  13.9 us (3%)
  starting transfers between devices  4.95 us (1%)
    all_gather x1, waiting for transfers between devices, expert_update(): part_rows = lax.all_gather(grads_pair, 'dp', axis=0, tiled=True)  130 us
    reduce_scatter x1, waiting for transfers between devices, weight_update(): lax.psum_scatter(lax.dot_general(query_grad, attn_input, (((0,), (0,)), (...  120 us
    reduce_scatter x1, waiting for transfers between devices, expert_update(): lax.psum_scatter(jnp.einsum('sec,ehc->seh', arrived, down_weight, preferr...  72.2 us
    all_to_all x1, blocking collectives, expert_update(): lax.all_to_all(outgoing, 'expert', split_axis=1, concat_axis=0, tiled=True)  37.3 us
    dot_general x1, matrix products, weight_update(): lax.dot_general(query_grad, attn_input, (((0,), (0,)), ((), ())), preferr...  11.8 us
  transfers between devices with their start and end apart: 4, of which 3 were waited for; matrix products, arithmetic and copies ran while one was open for 9% of the time, Pallas kernels for 0%

commit v1 on v0

v1 whole, which is shorter than its diff:
```python
import jax
import jax.numpy as jnp
from jax import lax
from jax.sharding import PartitionSpec as P

step_rate = 0.01
epsilon = 1e-06


def shift(value, n, hops, first, last):
    return lax.ppermute(value, "dp", [(i, i + hops) for i in range(first, last + 1) if 0 <= i + hops < n])


def ordered(z, lefts, rights):
    near = jnp.where(z <= 1, rights[0], lefts[0])
    middle = jnp.where(z == 0, rights[1], jnp.where(z == 1, lefts[0], jnp.where(z == 2, rights[0], lefts[1])))
    far = jnp.where(z == 0, rights[2], jnp.where(z == 1, rights[1], jnp.where(z == 2, lefts[1], lefts[2])))
    return near, middle, far


def ordered_sources(z):
    near = jnp.where(z <= 1, z + 1, z - 1)
    middle = jnp.where(z == 0, 2, jnp.where(z == 1, 0, jnp.where(z == 2, 3, 1)))
    far = jnp.where(z <= 1, 3, 0)
    return near, middle, far


def line_gather(value, n):
    lefts, rights = [], []
    from_left, from_right = value, value
    for step in range(n - 1):
        from_left = shift(from_left, n, 1, step, n - 2)
        from_right = shift(from_right, n, -1, 1, n - 1 - step)
        lefts.append(from_left)
        rights.append(from_right)
    return lefts, rights


def line_reduce_scatter(parts, n, z):
    def block(index):
        return lax.dynamic_index_in_dim(parts, jnp.clip(index, 0, n - 1), 0, keepdims=False)

    from_left = from_right = None
    for step in range(1, n):
        up = block(z + n - step)
        down = block(z - n + step)
        if from_left is not None:
            up = up + from_left.astype(jnp.float32)
            down = down + from_right.astype(jnp.float32)
        from_left = shift(up.astype(jnp.bfloat16), n, 1, 0, step - 1)
        from_right = shift(down.astype(jnp.bfloat16), n, -1, n - step, n - 1)
    return block(z) + from_left.astype(jnp.float32) + from_right.astype(jnp.float32)


def activation_grads(hidden, gate_vals, up_vals):
    gate_float = gate_vals.astype(jnp.float32)
    up_float = up_vals.astype(jnp.float32)
    sigmoid_vals = jax.nn.sigmoid(gate_float)
    gate_grad = hidden * up_float * sigmoid_vals * (1.0 + gate_float * (1.0 - sigmoid_vals))
    up_grad = hidden * gate_float * sigmoid_vals
    return jnp.stack([gate_grad, up_grad], axis=0).astype(jnp.bfloat16)


def row_update(query_weight, gradient):
    radial = jnp.mean(query_weight * gradient, axis=1, keepdims=True) / (
        jnp.mean(query_weight * query_weight, axis=1, keepdims=True) + epsilon
    )
    stepped = query_weight - step_rate * (gradient - radial * query_weight)
    return stepped * lax.rsqrt(jnp.mean(stepped * stepped, axis=1, keepdims=True) + epsilon)


def token_product(grads, inputs):
    return lax.dot_general(grads, inputs, (((0,), (0,)), ((), ())), preferred_element_type=jnp.float32)


def weight_update_scattered(attn_input, query_grad, query_weight):
    gradient = lax.psum_scatter(
        token_product(query_grad, attn_input).astype(jnp.bfloat16), "dp", scatter_dimension=0, tiled=True
    ).astype(jnp.float32)
    return row_update(query_weight, gradient)


def weight_update_gathered(attn_input, query_grad, query_weight):
    n = lax.axis_size("dp")
    z = lax.axis_index("dp")
    group = lax.axis_index("expert")
    rows = query_weight.shape[0]
    share = attn_input.shape[0] // lax.axis_size("expert")

    own_slice = lax.dynamic_slice_in_dim(attn_input, group * share, share, 0)
    slices = ordered(z, *line_gather(own_slice, n))

    def columns(index):
        return lax.dynamic_slice_in_dim(query_grad, jnp.clip(index, 0, n - 1) * rows, rows, 1)

    lefts = [shift(columns(z + k), n, k, 0, n - 1 - k) for k in range(1, n)]
    rights = [shift(columns(z - k), n, -k, k, n - 1) for k in range(1, n)]
    grads = ordered(z, lefts, rights)

    gradient = token_product(columns(z), attn_input)
    for grad, part in zip(grads, slices):
        whole = lax.all_gather(part, "expert", axis=0, tiled=True)
        gradient = gradient + token_product(grad, whole)
    return row_update(query_weight, gradient)


def expert_update(
    moe_cotangent,
    expert_ids,
    route_weights,
    gate_saved,
    up_saved,
    gate_weight,
    up_weight,
    down_weight,
):
    groups = lax.axis_size("expert")
    n = lax.axis_size("dp")
    z = lax.axis_index("dp")
    local = gate_weight.shape[0]
    per_dp = gate_saved.shape[0]
    capacity = per_dp * n // groups
    tokens, width = moe_cotangent.shape
    hidden_units = down_weight.shape[1]
    blocks = groups // n

    rows = lax.all_gather(moe_cotangent, "expert", axis=0, tiled=False)
    routing = lax.all_gather(
        jnp.concatenate([expert_ids.astype(jnp.float32), route_weights], axis=1), "expert", axis=0, tiled=False
    )
    top = expert_ids.shape[1]
    ids = routing[:, :, :top].astype(jnp.int32)
    weights = routing[:, :, top:]

    mine = lax.axis_index("expert") * local + lax.broadcasted_iota(jnp.int32, (1, local, 1, 1), 1)
    hit = ids[:, None] == mine
    chosen = jnp.any(hit, axis=3)
    counts = chosen.astype(jnp.int32)
    token_weight = jnp.sum(jnp.where(hit, weights[:, None], 0.0), axis=3)
    position = jnp.cumsum(counts, axis=2, dtype=jnp.int32) - counts
    slot = jnp.where(chosen, position, -1)
    slot_iota = lax.broadcasted_iota(jnp.int32, (1, 1, capacity, 1), 2)
    matched = slot[:, :, None, :] == slot_iota
    select = matched.astype(jnp.bfloat16)
    slot_weight = jnp.sum(jnp.where(matched, token_weight[:, :, None, :], 0.0), axis=3)

    arrived = jnp.einsum("gect,gtd->gecd", select, rows, preferred_element_type=jnp.float32)
    arrived = (arrived * slot_weight[..., None]).astype(jnp.bfloat16)
    arrived = jnp.transpose(arrived, (1, 0, 2, 3)).reshape(local, groups * capacity, width)

    gathered = []
    for expert in range(local):
        parts = jnp.einsum(
            "sd,hd->sh", arrived[expert], down_weight[expert], preferred_element_type=jnp.float32
        )
        if n == 4:
            parts = parts.astype(jnp.bfloat16).reshape(n, per_dp, hidden_units).astype(jnp.float32)
            hidden = line_reduce_scatter(parts, n, z)
        else:
            hidden = lax.psum_scatter(
                parts.astype(jnp.bfloat16), "dp", scatter_dimension=0, tiled=True
            ).astype(jnp.float32)
        grads = activation_grads(hidden, gate_saved[:, expert], up_saved[:, expert])
        if n == 4:
            gathered.append((grads,) + ordered(z, *line_gather(grads, n)))
        else:
            gathered.append((lax.all_gather(grads, "dp", axis=1, tiled=True),))

    sources = (z,) + ordered_sources(z) if n == 4 else (0,)
    chunk = per_dp // capacity if n == 4 else groups
    returned = jnp.zeros((groups, tokens, width), jnp.bfloat16)
    for place, source in enumerate(sources):
        total = 0.0
        first = source * chunk
        chunk_select = lax.dynamic_slice_in_dim(select, first, chunk, 0)
        for expert in range(local):
            grads = gathered[expert][place]
            slot_input = jnp.einsum("sh,ch->sc", grads[0], gate_weight[expert], preferred_element_type=jnp.float32)
            slot_input = slot_input + jnp.einsum(
                "sh,ch->sc", grads[1], up_weight[expert], preferred_element_type=jnp.float32
            )
            slot_input = slot_input.astype(jnp.bfloat16).reshape(chunk, capacity, width)
            total = total + jnp.einsum(
                "gct,gcd->gtd", chunk_select[:, expert], slot_input, preferred_element_type=jnp.float32
            )
        returned = lax.dynamic_update_slice_in_dim(returned, total.astype(jnp.bfloat16), first, 0)
    return lax.psum_scatter(returned, "expert", scatter_dimension=0, tiled=False).astype(jnp.float32)


def shards(
    attn_input,
    query_grad,
    query_weight,
    moe_cotangent,
    expert_ids,
    route_weights,
    gate_saved,
    up_saved,
    gate_weight,
    up_weight,
    down_weight,
):
    moe_input_grad = expert_update(
        moe_cotangent,
        expert_ids,
        route_weights,
        gate_saved,
        up_saved,
        gate_weight,
        up_weight,
        down_weight,
    )
    update = weight_update_gathered if lax.axis_size("dp") == 4 else weight_update_scattered
    query_weight_next = update(attn_input, query_grad, query_weight)
    return (query_weight_next, moe_input_grad)


def solution(mesh):
    placed = (
        P("dp", None),
        P("dp", "expert"),
        P(("expert", "dp"), None),
        P("expert", "dp"),
        P("expert", None),
        P("expert", None),
        P("dp", "expert", None),
        P("dp", "expert", None),
        P("expert", "dp", None),
        P("expert", "dp", None),
        P("expert", None, "dp"),
    )
    return jax.shard_map(
        shards,
        mesh=mesh,
        in_specs=placed,
        out_specs=(P(("expert", "dp"), None), P("expert", "dp")),
        check_vma=False,
    )
```

time: 456 us -> 504 us (1.11); the launches traced: 455 us -> 494 us
  starting transfers between devices: 4.95 us -> 90.1 us
  waiting for transfers between devices: 322 us -> 269 us
  blocking collectives: 37.3 us -> 10.5 us
  matrix products: 39.6 us -> 65.3 us
  other arithmetic: 17.9 us -> 31.5 us
  local copies, waits for them, and re-layouts: 19.3 us -> 12.7 us
    reduce_scatter x2 -> x1, waiting for transfers between devices: 192 us -> 0.01 us  [expert_update(): lax.psum_scatter(returned, 'expert', scatter_dimension=0, tiled=False)]
    ppermute x0 -> x36, waiting for transfers between devices: none -> 157 us  [shift(): lax.ppermute(value, 'dp', [(i, i + hops) for i in range(first, last + 1)...]
    ppermute x0 -> x36, starting transfers between devices: none -> 89.9 us  [shift(): lax.ppermute(value, 'dp', [(i, i + hops) for i in range(first, last + 1)...]
    all_to_all x1 -> x0, blocking collectives: 37.3 us -> none  [expert_update(): lax.all_to_all(outgoing, 'expert', split_axis=1, concat_axis=0, tiled=True)]
    dot_general x6 -> x31, matrix products: 39.6 us -> 65.3 us  [the longest x4 30.7 us: token_product(): lax.dot_general(grads, inputs, (((0,), (0,)), ((), ())), preferred_elemen...]
    all_gather x1 -> x4, waiting for transfers between devices: 130 us -> 110 us  [the longest x3 91.1 us: weight_update_gathered(): whole = lax.all_gather(part, 'expert', axis=0, tiled=True)]
    convert_element_type x0 -> x12, other arithmetic: none -> 13.3 us  [the longest x4 6.23 us: line_reduce_scatter(): from_left = shift(up.astype(jnp.bfloat16), n, 1, 0, step - 1)]
    all_gather x0 -> x1, blocking collectives: none -> 10.5 us  [expert_update(): lax.all_gather(jnp.concatenate([expert_ids.astype(jnp.float32), route_wei...]
  transfers between devices with their start and end apart: 4 -> 41, of which waited for: 3 -> 19; matrix products, arithmetic and copies ran while one was open for 9% -> 17% of each run, Pallas kernels for 0% -> 0%
where the time goes in v1:
time: 504 us; the launch traced here: 494 us
  waiting for transfers between devices  269 us (53%)
  starting transfers between devices  90.1 us (18%)
  matrix products  65.3 us (13%)
  other arithmetic  31.5 us (6%)
  between operations  15 us (3%)
  local copies, waits for them, and re-layouts  12.7 us (3%)
  blocking collectives  10.5 us (2%)
    ppermute x36, waiting for transfers between devices, shift(): lax.ppermute(value, 'dp', [(i, i + hops) for i in range(first, last + 1)...  157 us
    all_gather x3, waiting for transfers between devices, weight_update_gathered(): whole = lax.all_gather(part, 'expert', axis=0, tiled=True)  91.1 us
    ppermute x36, starting transfers between devices, shift(): lax.ppermute(value, 'dp', [(i, i + hops) for i in range(first, last + 1)...  89.9 us
    dot_general x4, matrix products, token_product(): lax.dot_general(grads, inputs, (((0,), (0,)), ((), ())), preferred_elemen...  30.7 us
    all_gather x1, waiting for transfers between devices, expert_update(): rows = lax.all_gather(moe_cotangent, 'expert', axis=0, tiled=False)  19.4 us
    dot_general x8, matrix products, expert_update(): jnp.einsum('sh,ch->sc', grads[1], up_weight[expert], preferred_element_ty...  13.4 us
    dot_general x8, matrix products, expert_update(): jnp.einsum('sh,ch->sc', grads[0], gate_weight[expert], preferred_element_...  11.3 us
    all_gather x1, blocking collectives, expert_update(): lax.all_gather(jnp.concatenate([expert_ids.astype(jnp.float32), route_wei...  10.5 us
  transfers between devices with their start and end apart: 41, of which 19 were waited for; matrix products, arithmetic and copies ran while one was open for 17% of the time, Pallas kernels for 0%

profile of v1, /device:TPU:0, one launch (start us, length us, event | category | flops | bytes accessed | tf_op | source)
XLA Modules:
  0.0 493.8 jit_solution(8396532846756623991)
XLA Ops:
  9.3 10.5 %all-gather = f32[1024,16]{0,1:T(8,128)S(1)} all-gather(f32[128,16]{0,1:T(8,128)S(1)} %pad_maximum_fusion.2), channel_id=2, replica_groups=mesh['expert'=8,'dp'=4] {'expert'}, dimensions={0}, use_global_device_ids=true | all-gather | bytes 73728 | tf_op jit(solution)/shard_map/all_gather | solution.py:128
  21.1 19.4 %all-gather.13.cloned.1.call-done = bf16[1024,1024]{1,0:T(8,128)(2,1)} async-done(((bf16[128,1024]{1,0:T(8,128)(2,1)}), bf16[1024,1024]{1,0:T(8,128)(2,1)}) %all-gather.13.cloned.1.call-update) | async-done | bytes 2097168 | tf_op jit(solution)/shard_map/all_gather | solution.py:127
  46.8 3.4 collective-permute-start.12
  58.6 3.1 collective-permute-done.12
  62.6 5.2 %collective-permute-start.13 = (bf16[160,1536]{1,0:T(8,128)(2,1)}, bf16[160,1536]{1,0:T(8,128)(2,1)}, u32[]{:S(2)}, u32[]{:S(2)}) collective-permute-start(bf16[160,1536]{1,0:T(8,128)(2,1)} %fusion.135), channel_id=1, source_target_pairs={{0,1},{1,2},{4,5},{5,6},{8,9},{9,10},{12,13},{13,14},{16,17},{17,1... | collective-permute-start | bytes 1474568 | tf_op jit(solution)/shard_map/ppermute | solution.py:11
  73.9 4.5 collective-permute-start.19
  78.4 4.5 collective-permute-done.13
  86.3 5.0 %collective-permute-start.14 = (bf16[160,1536]{1,0:T(8,128)(2,1)}, bf16[160,1536]{1,0:T(8,128)(2,1)S(1)}, u32[]{:S(2)}, u32[]{:S(2)}) collective-permute-start(bf16[160,1536]{1,0:T(8,128)(2,1)} %get-tuple-element.12), channel_id=1, source_target_pairs={{0,1},{1,2},{2,3},{4,5},{5,6},{6,7},{8,9},{9,10},{10,11},{12,13},{... | collective-permute-start | bytes 1474568 | tf_op jit(solution)/shard_map/ppermute | solution.py:11
  101.7 9.6 %collective-permute-start.20 = (bf16[160,1536]{1,0:T(8,128)(2,1)}, bf16[160,1536]{1,0:T(8,128)(2,1)S(1)}, u32[]{:S(2)}, u32[]{:S(2)}) collective-permute-start(bf16[160,1536]{1,0:T(8,128)(2,1)} %get-tuple-element.8), channel_id=1, source_target_pairs={{0,1},{1,2},{2,3},{4,5},{5,6},{6,7},{8,9},{9,10},{10,11},{12,13},{... | collective-permute-start | bytes 1474568 | tf_op jit(solution)/shard_map/ppermute | solution.py:11
  120.2 12.7 %collective-permute-start.25 = (bf16[2,160,1536]{2,1,0:T(8,128)(2,1)}, bf16[2,160,1536]{2,1,0:T(8,128)(2,1)}, u32[]{:S(2)}, u32[]{:S(2)}) collective-permute-start(bf16[2,160,1536]{2,1,0:T(8,128)(2,1)} %pad_maximum_fusion), channel_id=1, source_target_pairs={{0,1},{1,2},{2,3},{4,5},{5,6},{6,7},{8,9},{9,10},{10,11},{12,13},{... | collective-permute-start | bytes 2949128 | tf_op jit(solution)/shard_map/ppermute | solution.py:11
  137.1 4.6 collective-permute-start.27
  141.7 11.0 %collective-permute-done.24 = bf16[2,160,1536]{2,1,0:T(8,128)(2,1)} collective-permute-done((bf16[2,160,1536]{2,1,0:T(8,128)(2,1)}, bf16[2,160,1536]{2,1,0:T(8,128)(2,1)}, u32[]{:S(2)}, u32[]{:S(2)}) %collective-permute-start.24) | collective-permute-done | bytes 983072 | tf_op jit(solution)/shard_map/ppermute | solution.py:11
  155.8 17.9 %collective-permute-done.26 = bf16[2,160,1536]{2,1,0:T(8,128)(2,1)S(1)} collective-permute-done((bf16[2,160,1536]{2,1,0:T(8,128)(2,1)}, bf16[2,160,1536]{2,1,0:T(8,128)(2,1)S(1)}, u32[]{:S(2)}, u32[]{:S(2)}) %collective-permute-start.26) | collective-permute-done | bytes 983072 | tf_op jit(solution)/shard_map/ppermute | solution.py:11
  180.2 3.4 fusion.25
  183.6 3.2 fusion.107
  186.8 8.0 %collective-permute-done.28 = bf16[2,160,1536]{2,1,0:T(8,128)(2,1)} collective-permute-done((bf16[2,160,1536]{2,1,0:T(8,128)(2,1)}, bf16[2,160,1536]{2,1,0:T(8,128)(2,1)}, u32[]{:S(2)}, u32[]{:S(2)}) %collective-permute-start.28) | collective-permute-done | bytes 983072 | tf_op jit(solution)/shard_map/ppermute | solution.py:11
  196.9 19.0 %collective-permute-done.30 = bf16[2,160,1536]{2,1,0:T(8,128)(2,1)} collective-permute-done((bf16[2,160,1536]{2,1,0:T(8,128)(2,1)S(1)}, bf16[2,160,1536]{2,1,0:T(8,128)(2,1)}, u32[]{:S(2)}, u32[]{:S(2)}) %collective-permute-start.30) | collective-permute-done | bytes 983072 | tf_op jit(solution)/shard_map/ppermute | solution.py:11
  223.2 30.5 %collective-permute-done.32 = bf16[2,160,1536]{2,1,0:T(8,128)(2,1)S(1)} collective-permute-done((bf16[2,160,1536]{2,1,0:T(8,128)(2,1)}, bf16[2,160,1536]{2,1,0:T(8,128)(2,1)S(1)}, u32[]{:S(2)}, u32[]{:S(2)}) %collective-permute-start.32) | collective-permute-done | bytes 983072 | tf_op jit(solution)/shard_map/ppermute | solution.py:11
  255.3 16.3 %collective-permute-done.34 = bf16[2,160,1536]{2,1,0:T(8,128)(2,1)S(1)} collective-permute-done((bf16[2,160,1536]{2,1,0:T(8,128)(2,1)}, bf16[2,160,1536]{2,1,0:T(8,128)(2,1)S(1)}, u32[]{:S(2)}, u32[]{:S(2)}) %collective-permute-start.34) | collective-permute-done | bytes 983072 | tf_op jit(solution)/shard_map/ppermute | solution.py:11
  294.4 16.5 %collective-permute-done.6 = bf16[96,4096]{1,0:T(8,128)(2,1)S(1)} collective-permute-done((bf16[96,4096]{1,0:T(8,128)(2,1)}, bf16[96,4096]{1,0:T(8,128)(2,1)S(1)}, u32[]{:S(2)}, u32[]{:S(2)}) %collective-permute-start.6) | collective-permute-done | bytes 786464 | tf_op jit(solution)/shard_map/ppermute | solution.py:11
  313.0 15.4 %collective-permute-done.10 = bf16[96,4096]{1,0:T(8,128)(2,1)S(1)} collective-permute-done((bf16[96,4096]{1,0:T(8,128)(2,1)S(1)}, bf16[96,4096]{1,0:T(8,128)(2,1)S(1)}, u32[]{:S(2)}, u32[]{:S(2)}) %collective-permute-start.10) | collective-permute-done | bytes 786464 | tf_op jit(solution)/shard_map/ppermute | solution.py:11
  336.3 5.5 %collective-permute-start.5 = (bf16[768,256]{1,0:T(8,128)(2,1)}, bf16[768,256]{1,0:T(8,128)(2,1)S(1)}, u32[]{:S(2)}, u32[]{:S(2)}) collective-permute-start(bf16[768,256]{1,0:T(8,128)(2,1)} %get-tuple-element.28), channel_id=1, source_target_pairs={{0,2},{1,3},{4,6},{5,7},{8,10},{9,11},{12,14},{13,15},{16,18},{17,... | collective-permute-start | bytes 1179656 | tf_op jit(solution)/shard_map/ppermute | solution.py:11
  343.1 6.4 %collective-permute-start.9 = (bf16[768,256]{1,0:T(8,128)(2,1)}, bf16[768,256]{1,0:T(8,128)(2,1)S(1)}, u32[]{:S(2)}, u32[]{:S(2)}) collective-permute-start(bf16[768,256]{1,0:T(8,128)(2,1)} %get-tuple-element.31), channel_id=1, source_target_pairs={{0,3},{4,7},{8,11},{12,15},{16,19},{20,23},{24,27},{28,31}} | collective-permute-start | bytes 1179656 | tf_op jit(solution)/shard_map/ppermute | solution.py:11
  349.5 6.6 %fusion.151 = f32[256,4096]{1,0:T(8,128)} fusion(bf16[768,4096]{1,0:T(8,128)(2,1)} %param.11, bf16[768,1024]{1,0:T(8,128)(2,1)S(1)} %copy-done.5, s32[]{:T(128)S(6)} %select_n.231), kind=kOutput, calls=%fused_computation.184 | convolution fusion | flops 1610612736 | bytes 10878980 | tf_op jit(solution)/shard_map/dot_general | solution.py:73
  357.9 8.3 %collective-permute-done.4 = bf16[768,256]{1,0:T(8,128)(2,1)S(1)} collective-permute-done((bf16[768,256]{1,0:T(8,128)(2,1)}, bf16[768,256]{1,0:T(8,128)(2,1)S(1)}, u32[]{:S(2)}, u32[]{:S(2)}) %collective-permute-start.4) | collective-permute-done | bytes 393248 | tf_op jit(solution)/shard_map/ppermute | solution.py:11
  367.8 10.7 %all-gather.11.cloned.1.call-done = bf16[768,4096]{1,0:T(8,128)(2,1)} async-done(((bf16[96,4096]{1,0:T(8,128)(2,1)}), bf16[768,4096]{1,0:T(8,128)(2,1)}) %all-gather.11.cloned.1.call-update) | async-done | bytes 6291472 | tf_op jit(solution)/shard_map/all_gather | solution.py:102
  378.5 6.7 %fusion.143 = f32[256,4096]{1,0:T(8,128)} fusion(bf16[768,4096]{1,0:T(8,128)(2,1)} %all-gather.11.cloned.1.call-done, bf16[768,256]{1,0:T(8,128)(2,1)S(1)} %collective-permute-done.8, bf16[768,256]{1,0:T(8,128)(2,1)S(1)} %collective-permute-done.4, bf16[768,256]{1,0:T(8,128)(2,1)S(1)} %collective-permute-done.5, ...), kind=kOutput, calls=%fused_computation.176 | convolution fusion | flops 1611202560 | bytes 12058627 | tf_op jit(solution)/shard_map/dot_general | solution.py:73
  385.1 40.8 %all-gather.7.cloned.1.call-done = bf16[768,4096]{1,0:T(8,128)(2,1)} async-done(((bf16[96,4096]{1,0:T(8,128)(2,1)}), bf16[768,4096]{1,0:T(8,128)(2,1)}) %all-gather.7.cloned.1.call-update) | async-done | bytes 6291472 | tf_op jit(solution)/shard_map/all_gather | solution.py:102
  425.9 7.9 %convolution_add_fusion.1 = f32[256,4096]{1,0:T(8,128)} fusion(f32[256,4096]{1,0:T(8,128)} %fusion.151, bf16[768,4096]{1,0:T(8,128)(2,1)} %all-gather.7.cloned.1.call-done, bf16[768,256]{1,0:T(8,128)(2,1)S(1)} %collective-permute-done, bf16[768,256]{1,0:T(8,128)(2,1)S(1)} %collective-permute-done.1, pred[]{:T(512)S(6)} %le.2), kind=kOutput, calls=%fused_computation.4 | convolution fusion | flops 1611857920 | bytes 15466497 | tf_op jit(solution)/shard_map/dot_general | solution.py:73
  433.8 39.6 %all-gather.9.cloned.1.call-done = bf16[768,4096]{1,0:T(8,128)(2,1)} async-done(((bf16[96,4096]{1,0:T(8,128)(2,1)}), bf16[768,4096]{1,0:T(8,128)(2,1)}) %all-gather.9.cloned.1.call-update) | async-done | bytes 6291472 | tf_op jit(solution)/shard_map/all_gather | solution.py:102
  473.4 9.5 %multiply_reduce_fusion.2 = (f32[256]{0:T(256)S(1)}, f32[256]{0:T(256)S(1)}, f32[256,4096]{1,0:T(8,128)S(1)}) fusion(f32[256,4096]{1,0:T(8,128)} %param.13, f32[256,4096]{1,0:T(8,128)} %fusion.143, f32[256,4096]{1,0:T(8,128)} %convolution_add_fusion.1, bf16[768,4096]{1,0:T(8,128)(2,1)} %all-gather.9.cloned.1.call-done, ...), kind=kOutput, calls=%fused_computation.8 | convolution fusion | flops 1617493504 | bytes 24643588 | tf_op jit(solution)/shard_map/dot_general | solution.py:73
  483.9 3.2 broadcast_multiply_fusion
  (170 shorter events, 109.8 us)
Async XLA Ops:
  7.2 33.4 %all-gather.13.cloned.1.call-start = ((), (), s32[]{:S(2)}) async-start(), calls=%async_computation.5 | async-start | bytes 2359296 | tf_op jit(solution)/shard_map/all_gather | solution.py:127
  7.9 348.3 %reduce-scatter.2.cloned.1.call-start = ((), (), s32[]{:S(2)}) async-start(), calls=%async_computation.4 | async-start | bytes 2359296 | tf_op jit(solution)/shard_map/reduce_scatter | solution.py:187
  50.3 28.2 %collective-permute-start.15 = (bf16[160,1536]{1,0:T(8,128)(2,1)S(1)}, bf16[160,1536]{1,0:T(8,128)(2,1)S(1)}, u32[]{:S(2)}, u32[]{:S(2)}) collective-permute-start(bf16[160,1536]{1,0:T(8,128)(2,1)S(1)} %get-tuple-element.15), channel_id=1, source_target_pairs={{3,2},{7,6},{11,10},{15,14},{19,18},{23,22},{27,26},{31,30}} | collective-permute-start | bytes 1474568 | tf_op jit(solution)/shard_map/ppermute | solution.py:11
  62.6 20.3 %collective-permute-start.13 = (bf16[160,1536]{1,0:T(8,128)(2,1)}, bf16[160,1536]{1,0:T(8,128)(2,1)}, u32[]{:S(2)}, u32[]{:S(2)}) collective-permute-start(bf16[160,1536]{1,0:T(8,128)(2,1)} %fusion.135), channel_id=1, source_target_pairs={{0,1},{1,2},{4,5},{5,6},{8,9},{9,10},{12,13},{13,14},{16,17},{17,1... | collective-permute-start | bytes 1474568 | tf_op jit(solution)/shard_map/ppermute | solution.py:11
  69.2 22.1 %collective-permute-start.21 = (bf16[160,1536]{1,0:T(8,128)(2,1)S(1)}, bf16[160,1536]{1,0:T(8,128)(2,1)S(1)}, u32[]{:S(2)}, u32[]{:S(2)}) collective-permute-start(bf16[160,1536]{1,0:T(8,128)(2,1)S(1)} %get-tuple-element.11), channel_id=1, source_target_pairs={{3,2},{7,6},{11,10},{15,14},{19,18},{23,22},{27,26},{31,30}} | collective-permute-start | bytes 1474568 | tf_op jit(solution)/shard_map/ppermute | solution.py:11
  73.9 19.5 %collective-permute-start.19 = (bf16[160,1536]{1,0:T(8,128)(2,1)S(1)}, bf16[160,1536]{1,0:T(8,128)(2,1)S(1)}, u32[]{:S(2)}, u32[]{:S(2)}) collective-permute-start(bf16[160,1536]{1,0:T(8,128)(2,1)S(1)} %fusion.130), channel_id=1, source_target_pairs={{0,1},{1,2},{4,5},{5,6},{8,9},{9,10},{12,13},{13,14},{16,17},{17,1... | collective-permute-start | bytes 1474568 | tf_op jit(solution)/shard_map/ppermute | solution.py:11
  86.3 27.8 %collective-permute-start.14 = (bf16[160,1536]{1,0:T(8,128)(2,1)}, bf16[160,1536]{1,0:T(8,128)(2,1)S(1)}, u32[]{:S(2)}, u32[]{:S(2)}) collective-permute-start(bf16[160,1536]{1,0:T(8,128)(2,1)} %get-tuple-element.12), channel_id=1, source_target_pairs={{0,1},{1,2},{2,3},{4,5},{5,6},{6,7},{8,9},{9,10},{10,11},{12,13},{... | collective-permute-start | bytes 1474568 | tf_op jit(solution)/shard_map/ppermute | solution.py:11
  101.7 31.3 %collective-permute-start.20 = (bf16[160,1536]{1,0:T(8,128)(2,1)}, bf16[160,1536]{1,0:T(8,128)(2,1)S(1)}, u32[]{:S(2)}, u32[]{:S(2)}) collective-permute-start(bf16[160,1536]{1,0:T(8,128)(2,1)} %get-tuple-element.8), channel_id=1, source_target_pairs={{0,1},{1,2},{2,3},{4,5},{5,6},{6,7},{8,9},{9,10},{10,11},{12,13},{... | collective-permute-start | bytes 1474568 | tf_op jit(solution)/shard_map/ppermute | solution.py:11
  112.8 20.2 %collective-permute-start.23 = (bf16[160,1536]{1,0:T(8,128)(2,1)S(1)}, bf16[160,1536]{1,0:T(8,128)(2,1)S(1)}, u32[]{:S(2)}, u32[]{:S(2)}) collective-permute-start(bf16[160,1536]{1,0:T(8,128)(2,1)S(1)} %fusion.129), channel_id=1, source_target_pairs={{1,0},{2,1},{3,2},{5,4},{6,5},{7,6},{9,8},{10,9},{11,10},{13,12},{... | collective-permute-start | bytes 1474568 | tf_op jit(solution)/shard_map/ppermute | solution.py:11
  119.0 33.7 %collective-permute-start.24 = (bf16[2,160,1536]{2,1,0:T(8,128)(2,1)}, bf16[2,160,1536]{2,1,0:T(8,128)(2,1)}, u32[]{:S(2)}, u32[]{:S(2)}) collective-permute-start(bf16[2,160,1536]{2,1,0:T(8,128)(2,1)} %pad_maximum_fusion), channel_id=1, source_target_pairs={{1,0},{2,1},{3,2},{5,4},{6,5},{7,6},{9,8},{10,9},{11,10},{13,12},{... | collective-permute-start | bytes 2949128 | tf_op jit(solution)/shard_map/ppermute | solution.py:11
  120.2 33.9 %collective-permute-start.25 = (bf16[2,160,1536]{2,1,0:T(8,128)(2,1)}, bf16[2,160,1536]{2,1,0:T(8,128)(2,1)}, u32[]{:S(2)}, u32[]{:S(2)}) collective-permute-start(bf16[2,160,1536]{2,1,0:T(8,128)(2,1)} %pad_maximum_fusion), channel_id=1, source_target_pairs={{0,1},{1,2},{2,3},{4,5},{5,6},{6,7},{8,9},{9,10},{10,11},{12,13},{... | collective-permute-start | bytes 2949128 | tf_op jit(solution)/shard_map/ppermute | solution.py:11
  135.8 37.8 %collective-permute-start.26 = (bf16[2,160,1536]{2,1,0:T(8,128)(2,1)}, bf16[2,160,1536]{2,1,0:T(8,128)(2,1)S(1)}, u32[]{:S(2)}, u32[]{:S(2)}) collective-permute-start(bf16[2,160,1536]{2,1,0:T(8,128)(2,1)} %pad_maximum_fusion.1), channel_id=1, source_target_pairs={{1,0},{2,1},{3,2},{5,4},{6,5},{7,6},{9,8},{10,9},{11,10},{13,12},{... | collective-permute-start | bytes 2949128 | tf_op jit(solution)/shard_map/ppermute | solution.py:11
  137.1 37.8 %collective-permute-start.27 = (bf16[2,160,1536]{2,1,0:T(8,128)(2,1)}, bf16[2,160,1536]{2,1,0:T(8,128)(2,1)S(1)}, u32[]{:S(2)}, u32[]{:S(2)}) collective-permute-start(bf16[2,160,1536]{2,1,0:T(8,128)(2,1)} %pad_maximum_fusion.1), channel_id=1, source_target_pairs={{0,1},{1,2},{2,3},{4,5},{5,6},{6,7},{8,9},{9,10},{10,11},{12,13},{... | collective-permute-start | bytes 2949128 | tf_op jit(solution)/shard_map/ppermute | solution.py:11
  152.7 42.1 %collective-permute-start.28 = (bf16[2,160,1536]{2,1,0:T(8,128)(2,1)}, bf16[2,160,1536]{2,1,0:T(8,128)(2,1)}, u32[]{:S(2)}, u32[]{:S(2)}) collective-permute-start(bf16[2,160,1536]{2,1,0:T(8,128)(2,1)} %collective-permute-done.24), channel_id=1, source_target_pairs={{1,0},{2,1},{5,4},{6,5},{9,8},{10,9},{13,12},{14,13},{17,16},{18,1... | collective-permute-start | bytes 2949128 | tf_op jit(solution)/shard_map/ppermute | solution.py:11
  154.2 42.0 %collective-permute-start.29 = (bf16[2,160,1536]{2,1,0:T(8,128)(2,1)}, bf16[2,160,1536]{2,1,0:T(8,128)(2,1)}, u32[]{:S(2)}, u32[]{:S(2)}) collective-permute-start(bf16[2,160,1536]{2,1,0:T(8,128)(2,1)} %collective-permute-done.25), channel_id=1, source_target_pairs={{1,2},{2,3},{5,6},{6,7},{9,10},{10,11},{13,14},{14,15},{17,18},{18... | collective-permute-start | bytes 2949128 | tf_op jit(solution)/shard_map/ppermute | solution.py:11
  173.7 42.2 %collective-permute-start.30 = (bf16[2,160,1536]{2,1,0:T(8,128)(2,1)S(1)}, bf16[2,160,1536]{2,1,0:T(8,128)(2,1)}, u32[]{:S(2)}, u32[]{:S(2)}) collective-permute-start(bf16[2,160,1536]{2,1,0:T(8,128)(2,1)S(1)} %collective-permute-done.26), channel_id=1, source_target_pairs={{1,0},{2,1},{5,4},{6,5},{9,8},{10,9},{13,12},{14,13},{17,16},{18,1... | collective-permute-start | bytes 2949128 | tf_op jit(solution)/shard_map/ppermute | solution.py:11
  175.0 42.2 %collective-permute-start.31 = (bf16[2,160,1536]{2,1,0:T(8,128)(2,1)S(1)}, bf16[2,160,1536]{2,1,0:T(8,128)(2,1)}, u32[]{:S(2)}, u32[]{:S(2)}) collective-permute-start(bf16[2,160,1536]{2,1,0:T(8,128)(2,1)S(1)} %collective-permute-done.27), channel_id=1, source_target_pairs={{1,2},{2,3},{5,6},{6,7},{9,10},{10,11},{13,14},{14,15},{17,18},{18... | collective-permute-start | bytes 2949128 | tf_op jit(solution)/shard_map/ppermute | solution.py:11
  178.7 113.5 %collective-permute-start.2 = (bf16[96,4096]{1,0:T(8,128)(2,1)}, bf16[96,4096]{1,0:T(8,128)(2,1)}, u32[]{:S(2)}, u32[]{:S(2)}) collective-permute-start(bf16[96,4096]{1,0:T(8,128)(2,1)} %constant_dynamic-slice_fusion.4), channel_id=1, source_target_pairs={{1,0},{2,1},{3,2},{5,4},{6,5},{7,6},{9,8},{10,9},{11,10},{13,12},{... | collective-permute-start | bytes 2359304 | tf_op jit(solution)/shard_map/ppermute | solution.py:11
  194.8 58.9 %collective-permute-start.32 = (bf16[2,160,1536]{2,1,0:T(8,128)(2,1)}, bf16[2,160,1536]{2,1,0:T(8,128)(2,1)S(1)}, u32[]{:S(2)}, u32[]{:S(2)}) collective-permute-start(bf16[2,160,1536]{2,1,0:T(8,128)(2,1)} %collective-permute-done.28), channel_id=1, source_target_pairs={{1,0},{5,4},{9,8},{13,12},{17,16},{21,20},{25,24},{29,28}} | collective-permute-start | bytes 2949128 | tf_op jit(solution)/shard_map/ppermute | solution.py:11
  196.1 59.2 %collective-permute-start.33 = (bf16[2,160,1536]{2,1,0:T(8,128)(2,1)}, bf16[2,160,1536]{2,1,0:T(8,128)(2,1)S(1)}, u32[]{:S(2)}, u32[]{:S(2)}) collective-permute-start(bf16[2,160,1536]{2,1,0:T(8,128)(2,1)} %collective-permute-done.29), channel_id=1, source_target_pairs={{2,3},{6,7},{10,11},{14,15},{18,19},{22,23},{26,27},{30,31}} | collective-permute-start | bytes 2949128 | tf_op jit(solution)/shard_map/ppermute | solution.py:11
  215.9 55.8 %collective-permute-start.34 = (bf16[2,160,1536]{2,1,0:T(8,128)(2,1)}, bf16[2,160,1536]{2,1,0:T(8,128)(2,1)S(1)}, u32[]{:S(2)}, u32[]{:S(2)}) collective-permute-start(bf16[2,160,1536]{2,1,0:T(8,128)(2,1)} %collective-permute-done.30), channel_id=1, source_target_pairs={{1,0},{5,4},{9,8},{13,12},{17,16},{21,20},{25,24},{29,28}} | collective-permute-start | bytes 2949128 | tf_op jit(solution)/shard_map/ppermute | solution.py:11
  217.2 54.5 %collective-permute-start.35 = (bf16[2,160,1536]{2,1,0:T(8,128)(2,1)}, bf16[2,160,1536]{2,1,0:T(8,128)(2,1)S(1)}, u32[]{:S(2)}, u32[]{:S(2)}) collective-permute-start(bf16[2,160,1536]{2,1,0:T(8,128)(2,1)} %collective-permute-done.31), channel_id=1, source_target_pairs={{2,3},{6,7},{10,11},{14,15},{18,19},{22,23},{26,27},{30,31}} | collective-permute-start | bytes 2949128 | tf_op jit(solution)/shard_map/ppermute | solution.py:11
  253.7 40.0 %collective-permute-start.3 = (bf16[96,4096]{1,0:T(8,128)(2,1)}, bf16[96,4096]{1,0:T(8,128)(2,1)S(1)}, u32[]{:S(2)}, u32[]{:S(2)}) collective-permute-start(bf16[96,4096]{1,0:T(8,128)(2,1)} %constant_dynamic-slice_fusion.4), channel_id=1, source_target_pairs={{0,1},{1,2},{2,3},{4,5},{5,6},{6,7},{8,9},{9,10},{10,11},{12,13},{... | collective-permute-start | bytes 2359304 | tf_op jit(solution)/shard_map/ppermute | solution.py:11
  292.2 86.2 %all-gather.11.cloned.1.call-start = ((), (), s32[]{:S(2)}) async-start(), calls=%async_computation.3 | async-start | bytes 7077888 | tf_op jit(solution)/shard_map/all_gather | solution.py:102
  331.1 94.9 %all-gather.7.cloned.1.call-start = ((), (), s32[]{:S(2)}) async-start(), calls=%async_computation.1 | async-start | bytes 7077888 | tf_op jit(solution)/shard_map/all_gather | solution.py:102
  331.6 141.7 %all-gather.9.cloned.1.call-start = ((), (), s32[]{:S(2)}) async-start(), calls=%async_computation.2 | async-start | bytes 7077888 | tf_op jit(solution)/shard_map/all_gather | solution.py:102
  333.7 51.4 %collective-permute-start = (bf16[768,256]{1,0:T(8,128)(2,1)}, bf16[768,256]{1,0:T(8,128)(2,1)S(1)}, u32[]{:S(2)}, u32[]{:S(2)}) collective-permute-start(bf16[768,256]{1,0:T(8,128)(2,1)} %get-tuple-element.30), channel_id=1, source_target_pairs={{1,0},{2,1},{3,2},{5,4},{6,5},{7,6},{9,8},{10,9},{11,10},{13,12},{... | collective-permute-start | bytes 1179656 | tf_op jit(solution)/shard_map/ppermute | solution.py:11
  335.0 31.2 %collective-permute-start.4 = (bf16[768,256]{1,0:T(8,128)(2,1)}, bf16[768,256]{1,0:T(8,128)(2,1)S(1)}, u32[]{:S(2)}, u32[]{:S(2)}) collective-permute-start(bf16[768,256]{1,0:T(8,128)(2,1)} %get-tuple-element.29), channel_id=1, source_target_pairs={{2,0},{3,1},{6,4},{7,5},{10,8},{11,9},{14,12},{15,13},{18,16},{19,... | collective-permute-start | bytes 1179656 | tf_op jit(solution)/shard_map/ppermute | solution.py:11
  336.3 31.4 %collective-permute-start.5 = (bf16[768,256]{1,0:T(8,128)(2,1)}, bf16[768,256]{1,0:T(8,128)(2,1)S(1)}, u32[]{:S(2)}, u32[]{:S(2)}) collective-permute-start(bf16[768,256]{1,0:T(8,128)(2,1)} %get-tuple-element.28), channel_id=1, source_target_pairs={{0,2},{1,3},{4,6},{5,7},{8,10},{9,11},{12,14},{13,15},{16,18},{17,... | collective-permute-start | bytes 1179656 | tf_op jit(solution)/shard_map/ppermute | solution.py:11
  341.8 25.9 %collective-permute-start.8 = (bf16[768,256]{1,0:T(8,128)(2,1)}, bf16[768,256]{1,0:T(8,128)(2,1)S(1)}, u32[]{:S(2)}, u32[]{:S(2)}) collective-permute-start(bf16[768,256]{1,0:T(8,128)(2,1)} %get-tuple-element.32), channel_id=1, source_target_pairs={{3,0},{7,4},{11,8},{15,12},{19,16},{23,20},{27,24},{31,28}} | collective-permute-start | bytes 1179656 | tf_op jit(solution)/shard_map/ppermute | solution.py:11
  343.1 24.6 %collective-permute-start.9 = (bf16[768,256]{1,0:T(8,128)(2,1)}, bf16[768,256]{1,0:T(8,128)(2,1)S(1)}, u32[]{:S(2)}, u32[]{:S(2)}) collective-permute-start(bf16[768,256]{1,0:T(8,128)(2,1)} %get-tuple-element.31), channel_id=1, source_target_pairs={{0,3},{4,7},{8,11},{12,15},{16,19},{20,23},{24,27},{28,31}} | collective-permute-start | bytes 1179656 | tf_op jit(solution)/shard_map/ppermute | solution.py:11
  366.2 18.9 %collective-permute-start.1 = (bf16[768,256]{1,0:T(8,128)(2,1)}, bf16[768,256]{1,0:T(8,128)(2,1)S(1)}, u32[]{:S(2)}, u32[]{:S(2)}) collective-permute-start(bf16[768,256]{1,0:T(8,128)(2,1)} %get-tuple-element.27), channel_id=1, source_target_pairs={{0,1},{1,2},{2,3},{4,5},{5,6},{6,7},{8,9},{9,10},{10,11},{12,13},{... | collective-permute-start | bytes 1179656 | tf_op jit(solution)/shard_map/ppermute | solution.py:11
  (28 other events, 608.8 us)
Sparse Core Ops, SparseCore 0:
  9.9 30.5 all-gather.12
  292.3 38.4 reduce-scatter.1
  332.9 45.5 all-gather.10
  380.4 45.5 all-gather.6
  427.8 45.5 all-gather.8
